TPU v7x, 512 devices: a whole 4x8x8 slice. The times are simulated.
512 devices in a mesh: dp: 16 (over z_lo, x), zero: 32 (over y, z_hi, core).
Axes of the slice: x: 4, y: 8, z: 8 (z_hi: 2, z_lo: 4; z = z_hi * 4 + z_lo), core: 2. Of those that a mesh axis runs over, the one named last changes fastest.
Arguments:
- gate_up: bfloat16 [2, 4096, 14336], P(None, 'dp', 'zero'), may hold values from -6 to 6
- cot_mean: bfloat16 [4096, 4096], P('dp', 'zero'), may hold values from -6 to 6
- label_rows: bfloat16 [64, 4096], P(None, 'dp'), may hold values from -6 to 6
- true_labels: int32 [4096], P('dp'), may hold values from 0 to 63
- sampled_labels: int32 [4096], P('dp'), may hold values from 0 to 63
- weight: bfloat16 [14336, 4096], P('zero', 'dp'), may hold values from -4 to 4
- moment: bfloat16 [14336, 4096], P('zero', 'dp'), may hold values from -0.29882812 to 0.29882812
- curvature: bfloat16 [14336, 4096], P('zero', 'dp'), may hold values from 0.0099487305 to 1
- bits: int32 [14336, 4096], P('zero', 'dp'), may hold values from 0 to 16383
Outputs:
- new_weight: bfloat16 [14336, 4096], P('zero')
- new_moment: bfloat16 [14336, 4096], P('zero', 'dp')
- new_curvature: bfloat16 [14336, 4096], P('zero', 'dp')
All inputs are finite; a program needn't handle non-finite values.
Results may differ from a plain program's by a relative error of at most 0.014.
Values may be sent and summed in bfloat16 or wider, within the bound.
A program may use at most 64 MiB of HBM per device.

v0:
```python
import math
import jax
import jax.numpy as jnp
from jax import lax
from jax.sharding import PartitionSpec as P

beta_one = 0.965
beta_two = 0.99
gamma_rate = 0.5
learn_rate = 0.05
decay_rate = 0.1


def dither(value, noise):
    return (value * (1.0 + (noise - 0.5) / 8.0)).astype(jnp.bfloat16)


def on_device(
    gate_up, cot_mean, label_rows, true_labels, sampled_labels, weight, moment, curvature, bits
):
    tok_rows = gate_up.shape[1]
    cands = label_rows.shape[0]
    groups = lax.axis_size("dp")
    factor = 1.0 / math.sqrt(tok_rows * groups)
    gate_part = gate_up[0].astype(jnp.float32)
    up_part = gate_up[1].astype(jnp.float32)
    hidden = (jax.nn.silu(gate_part) * up_part).astype(jnp.bfloat16)
    classes = jnp.arange(cands, dtype=jnp.int32)
    hot_true = (true_labels[:, None] == classes[None, :]).astype(jnp.bfloat16)
    hot_sampled = (sampled_labels[:, None] == classes[None, :]).astype(jnp.bfloat16)
    label_part = jnp.dot(
        hidden.T,
        jnp.concatenate([hot_true, hot_sampled], axis=1),
        preferred_element_type=jnp.float32,
    )
    label_total = lax.psum(label_part.astype(jnp.bfloat16), "dp").astype(jnp.float32)
    terms = jnp.dot(
        hidden.T,
        lax.all_gather(cot_mean, "zero", axis=1, tiled=True),
        preferred_element_type=jnp.float32,
    )
    owned = lax.psum_scatter(
        terms.astype(jnp.bfloat16), "dp", scatter_dimension=1, tiled=True
    ).astype(jnp.float32)
    label_wide = label_rows.astype(jnp.float32)
    grad_true = (
        owned - jnp.dot(label_total[:, :cands], label_wide, precision=lax.Precision.HIGHEST)
    ) * factor
    grad_sampled = (
        owned - jnp.dot(label_total[:, cands:], label_wide, precision=lax.Precision.HIGHEST)
    ) * factor
    low_bits = bits % 128
    high_bits = bits // 128
    noise_one = (low_bits.astype(jnp.float32) + 0.5) / 128.0
    noise_two = (high_bits.astype(jnp.float32) + 0.5) / 128.0
    noise_three = (((3 * low_bits + 5 * high_bits) % 128).astype(jnp.float32) + 0.5) / 128.0
    new_moment = dither(
        beta_one * moment.astype(jnp.float32) + (1.0 - beta_one) * grad_true, noise_one
    )
    new_curvature = dither(
        beta_two * curvature.astype(jnp.float32) + (1.0 - beta_two) * grad_sampled * grad_sampled,
        noise_two,
    )
    ratio = jnp.clip(
        new_moment.astype(jnp.float32) / (gamma_rate * new_curvature.astype(jnp.float32)), -1.0, 1.0
    )
    shrunk = weight.astype(jnp.float32) * (1.0 - learn_rate * decay_rate) - learn_rate * ratio
    weight_piece = dither(shrunk, noise_three)
    new_weight = lax.all_gather(weight_piece, "dp", axis=1, tiled=True)
    return (new_weight, new_moment, new_curvature)


def solution(mesh):
    in_specs = (
        P(None, "dp", "zero"),
        P("dp", "zero"),
        P(None, "dp"),
        P("dp"),
        P("dp"),
        P("zero", "dp"),
        P("zero", "dp"),
        P("zero", "dp"),
        P("zero", "dp"),
    )
    out_specs = (P("zero", None), P("zero", "dp"), P("zero", "dp"))
    return jax.shard_map(
        on_device, mesh=mesh, in_specs=in_specs, out_specs=out_specs, check_vma=False
    )
```

profile of v0, /device:TPU:4, one launch (start us, length us, event | category | flops | bytes accessed | tf_op | source)
XLA Modules:
  0.0 387.3 jit_solution(16972792300468119694)
XLA Ops:
  8.0 0.0 copy-start
  8.0 0.0 all-gather.3.cloned.1.call-start
  8.1 0.7 all-gather.3.cloned.1.call-update
  8.7 0.0 all-reduce.2.cloned.1.call-start
  8.8 0.8 iota_compare_fusion
  9.6 1.2 fusion.17
  10.8 0.9 convolution_convert_fusion.1
  11.8 0.0 all-reduce.2.cloned.1.call-update
  11.8 0.0 copy-start.1
  11.8 0.0 copy-start.2
  11.8 0.0 reduce-scatter.2.cloned.1.call-start
  11.9 99.6 %all-gather.3.cloned.1.call-done = bf16[256,4096]{1,0:T(8,128)(2,1)} async-done(((bf16[256,128]{1,0:T(8,128)(2,1)}), bf16[256,4096]{1,0:T(8,128)(2,1)}) %all-gather.3.cloned.1.call-update) | async-done | bytes 2097168 | tf_op jit(solution)/shard_map/all_gather | solution.py:39
  111.4 4.6 %convolution_convert_fusion = bf16[448,4096]{1,0:T(8,128)(2,1)} fusion(bf16[256,448]{0,1:T(8,128)(2,1)S(1)} %fusion.17, bf16[256,4096]{1,0:T(8,128)(2,1)} %all-gather.3.cloned.1.call-done), kind=kOutput, calls=%fused_computation | convolution fusion | flops 941359104 | bytes 5996544 | tf_op jit(solution)/shard_map/dot_general | solution.py:37
  116.0 0.0 reduce-scatter.2.cloned.1.call-update
  116.0 0.0 all-gather.5.cloned.1.call-start
  116.1 67.2 %all-reduce.2.cloned.1.call-done = bf16[448,128]{1,0:T(8,128)(2,1)} async-done(((bf16[448,128]{1,0:T(8,128)(2,1)}), bf16[448,128]{1,0:T(8,128)(2,1)}) %all-reduce.2.cloned.1.call-update) | async-done | bytes 114704 | tf_op jit(solution)/shard_map/psum | solution.py:36
  183.2 96.9 %reduce-scatter.2.cloned.1.call-done = bf16[448,256]{1,0:T(8,128)(2,1)} async-done(((bf16[448,4096]{1,0:T(8,128)(2,1)}), bf16[448,256]{1,0:T(8,128)(2,1)}) %reduce-scatter.2.cloned.1.call-update) | async-done | bytes 229392 | tf_op jit(solution)/shard_map/reduce_scatter | solution.py:42
  280.2 0.0 copy-done.1
  280.2 1.4 fusion.3
  281.6 0.0 copy-start.5
  281.7 3.0 fusion.16
  284.7 0.0 all-gather.5.cloned.1.call-update
  284.7 90.7 %all-gather.5.cloned.1.call-done = bf16[448,4096]{1,0:T(8,128)(2,1)} async-done(((bf16[448,256]{1,0:T(8,128)(2,1)}), bf16[448,4096]{1,0:T(8,128)(2,1)}) %all-gather.5.cloned.1.call-update) | async-done | bytes 3670032 | tf_op jit(solution)/shard_map/all_gather | solution.py:69
  375.4 4.3 %copy.18 = bf16[448,4096]{1,0:T(8,128)(2,1)} copy(bf16[448,4096]{1,0:T(8,128)(2,1)} %all-gather.5.cloned.1.call-done) | data formatting | bytes 7340032
  (7 shorter events, 0.0 us)
Async XLA Ops:
  8.0 272.2 %copy-start = (bf16[64,256]{1,0:T(8,128)(2,1)S(1)}, bf16[64,256]{1,0:T(8,128)(2,1)}, u32[]{:S(2)}) copy-start(bf16[64,256]{1,0:T(8,128)(2,1)} %param.11) | copy-start | bytes 98308
  8.0 103.4 %all-gather.3.cloned.1.call-start = ((), (), s32[]{:S(2)}) async-start(), calls=%async_computation.1 | async-start | bytes 2162688 | tf_op jit(solution)/shard_map/all_gather | solution.py:39
  8.7 174.5 %all-reduce.2.cloned.1.call-start = ((), (), s32[]{:S(2)}) async-start(), calls=%async_computation.3 | async-start | bytes 229376 | tf_op jit(solution)/shard_map/psum | solution.py:36
  11.8 268.4 %copy-start.1 = (s32[448,256]{1,0:T(8,128)S(1)}, s32[448,256]{1,0:T(8,128)}, u32[]{:S(2)}) copy-start(s32[448,256]{1,0:T(8,128)} %param.17) | copy-start | bytes 1376260
  11.8 268.4 %copy-start.2 = (bf16[448,256]{1,0:T(8,128)(2,1)S(1)}, bf16[448,256]{1,0:T(8,128)(2,1)}, u32[]{:S(2)}) copy-start(bf16[448,256]{1,0:T(8,128)(2,1)} %param.15) | copy-start | bytes 688132
  11.8 268.3 %reduce-scatter.2.cloned.1.call-start = ((), (), s32[]{:S(2)}) async-start(), calls=%async_computation.2 | async-start | bytes 3899392 | tf_op jit(solution)/shard_map/reduce_scatter | solution.py:42
  116.0 165.6 %copy-start.3 = (bf16[448,256]{1,0:T(8,128)(2,1)S(1)}, bf16[448,256]{1,0:T(8,128)(2,1)}, u32[]{:S(2)}) copy-start(bf16[448,256]{1,0:T(8,128)(2,1)} %param.14) | copy-start | bytes 688132
  116.0 165.6 %copy-start.4 = (bf16[448,256]{1,0:T(8,128)(2,1)S(1)}, bf16[448,256]{1,0:T(8,128)(2,1)}, u32[]{:S(2)}) copy-start(bf16[448,256]{1,0:T(8,128)(2,1)} %param.16) | copy-start | bytes 688132
  116.0 259.4 %all-gather.5.cloned.1.call-start = ((), (), s32[]{:S(2)}) async-start(), calls=%async_computation.4 | async-start | bytes 3899392 | tf_op jit(solution)/shard_map/all_gather | solution.py:69
  281.6 3.1 copy-start.5
Sparse Core Ops, SparseCore 0:
  12.5 98.9 all-gather.2
Sparse Core Ops, SparseCore 1:
  12.7 170.5 all-reduce.1
  186.8 93.3 reduce-scatter.1
  284.8 90.5 all-gather.4
where the time goes:
time: 388 us; the launch traced here: 387 us
  waiting for transfers between devices  355 us (91%)
  between operations  15.7 us (4%)
  matrix products  9.97 us (3%)
  local copies, waits for them, and re-layouts  4.33 us (1%)
    all_gather x1, waiting for transfers between devices, on_device(): lax.all_gather(cot_mean, 'zero', axis=1, tiled=True)  99.6 us
    reduce_scatter x1, waiting for transfers between devices, on_device(): lax.psum_scatter(terms.astype(jnp.bfloat16), 'dp', scatter_dimension=1, t...  96.9 us
    all_gather x1, waiting for transfers between devices, on_device(): new_weight = lax.all_gather(weight_piece, 'dp', axis=1, tiled=True)  90.7 us
    psum x1, waiting for transfers between devices, on_device(): lax.psum(label_part.astype(jnp.bfloat16), 'dp').astype(jnp.float32)  67.2 us
  transfers between devices with their start and end apart: 4, of which 4 were waited for; matrix products, arithmetic and copies ran while one was open for 2% of the time, Pallas kernels for 0%

commit v1 on v0

--- a/solution.py
+++ b/solution.py
@@ -36,7 +36,9 @@
     label_total = lax.psum(label_part.astype(jnp.bfloat16), "dp").astype(jnp.float32)
     terms = jnp.dot(
         hidden.T,
-        lax.all_gather(cot_mean, "zero", axis=1, tiled=True),
+        jnp.concatenate(
+            lax.all_to_all(jnp.stack([cot_mean] * lax.axis_size("zero")), "zero", 0, 0), axis=1
+        ),
         preferred_element_type=jnp.float32,
     )
     owned = lax.psum_scatter(

time: 388 us -> 417 us (1.075)
  waiting for transfers between devices: 355 us -> 372 us
  starting transfers between devices: 0.17 us -> 16.1 us
    all_gather x1 -> x0, waiting for transfers between devices: 99.6 us -> none  [on_device(): lax.all_gather(cot_mean, 'zero', axis=1, tiled=True)]
    psum x1, waiting for transfers between devices: 67.2 us -> 129 us  [on_device(): lax.psum(label_part.astype(jnp.bfloat16), 'dp').astype(jnp.float32)]
    all_to_all x0 -> x1, waiting for transfers between devices: none -> 53.9 us  [on_device(): lax.all_to_all(jnp.stack([cot_mean] * lax.axis_size('zero')), 'zero', 0, 0)]
    all_to_all x0 -> x1, starting transfers between devices: none -> 15.9 us  [on_device(): lax.all_to_all(jnp.stack([cot_mean] * lax.axis_size('zero')), 'zero', 0, 0)]
  transfers between devices with their start and end apart: 4 -> 4, of which waited for: 4 -> 4; matrix products, arithmetic and copies ran while one was open for 2% -> 1% of each run, Pallas kernels for 0% -> 0%
where the time goes in v1:
time: 417 us
  waiting for transfers between devices  372 us (89%)
  starting transfers between devices  16.1 us (4%)
  between operations  13.9 us (3%)
  matrix products  8.46 us (2%)
  local copies, waits for them, and re-layouts  6.89 us (2%)
    psum x1, waiting for transfers between devices, on_device(): lax.psum(label_part.astype(jnp.bfloat16), 'dp').astype(jnp.float32)  129 us
    reduce_scatter x1, waiting for transfers between devices, on_device(): lax.psum_scatter(terms.astype(jnp.bfloat16), 'dp', scatter_dimension=1, t...  97 us
    all_gather x1, waiting for transfers between devices, on_device(): new_weight = lax.all_gather(weight_piece, 'dp', axis=1, tiled=True)  91.2 us
    all_to_all x1, waiting for transfers between devices, on_device(): lax.all_to_all(jnp.stack([cot_mean] * lax.axis_size('zero')), 'zero', 0, 0)  53.9 us
    all_to_all x1, starting transfers between devices, on_device(): lax.all_to_all(jnp.stack([cot_mean] * lax.axis_size('zero')), 'zero', 0, 0)  15.9 us
  transfers between devices with their start and end apart: 4, of which 4 were waited for; matrix products, arithmetic and copies ran while one was open for 1% of the time, Pallas kernels for 0%

profile of v1, /device:TPU:4, one launch (start us, length us, event | category | flops | bytes accessed | tf_op | source)
XLA Modules:
  0.0 417.1 jit_solution(14103303800977296007)
XLA Ops:
  7.2 0.0 copy-start
  7.2 0.0 copy-start.1
  7.2 1.0 copy.12
  8.2 1.6 stack.2
  9.8 15.9 %all-to-all-start = ((bf16[32,256,128]{1,2,0:T(8,128)(2,1)}), bf16[32,256,128]{1,2,0:T(8,128)(2,1)S(1)}, u32[]{:S(2)}, u32[]{:S(2)}) async-start(bf16[32,256,128]{1,2,0:T(8,128)(2,1)} %stack.2), calls=%async_computation | async-start | bytes 4194304 | tf_op jit(solution)/shard_map/all_to_all | solution.py:40
  25.7 0.0 all-reduce.2.cloned.1.call-start
  25.8 0.1 iota_compare_fusion
  25.9 1.0 convolution_convert_fusion.1
  26.9 0.0 all-reduce.2.cloned.1.call-update
  26.9 0.0 reduce-scatter.2.cloned.1.call-start
  27.0 53.9 %all-to-all-done = bf16[32,256,128]{1,2,0:T(8,128)(2,1)S(1)} async-done(((bf16[32,256,128]{1,2,0:T(8,128)(2,1)}), bf16[32,256,128]{1,2,0:T(8,128)(2,1)S(1)}, u32[]{:S(2)}, u32[]{:S(2)}) %all-to-all-start) | async-done | bytes 2097184 | tf_op jit(solution)/shard_map/all_to_all | solution.py:40
  80.9 3.0 convolution_convert_fusion
  83.9 0.0 reduce-scatter.2.cloned.1.call-update
  84.0 0.0 all-gather.2.cloned.1.call-start
  84.0 129.4 %all-reduce.2.cloned.1.call-done = bf16[448,128]{1,0:T(8,128)(2,1)} async-done(((bf16[448,128]{1,0:T(8,128)(2,1)}), bf16[448,128]{1,0:T(8,128)(2,1)}) %all-reduce.2.cloned.1.call-update) | async-done | bytes 114704 | tf_op jit(solution)/shard_map/psum | solution.py:36
  213.4 97.0 %reduce-scatter.2.cloned.1.call-done = bf16[448,256]{1,0:T(8,128)(2,1)} async-done(((bf16[448,4096]{1,0:T(8,128)(2,1)}), bf16[448,256]{1,0:T(8,128)(2,1)}) %reduce-scatter.2.cloned.1.call-update) | async-done | bytes 229392 | tf_op jit(solution)/shard_map/reduce_scatter | solution.py:44
  310.5 0.0 copy-done
  310.5 1.4 fusion.3
  311.9 0.0 copy-start.8
  312.0 3.0 fusion.23
  315.0 0.0 copy-done.8
  315.0 0.0 all-gather.2.cloned.1.call-update
  315.0 91.2 %all-gather.2.cloned.1.call-done = bf16[448,4096]{1,0:T(8,128)(2,1)} async-done(((bf16[448,256]{1,0:T(8,128)(2,1)}), bf16[448,4096]{1,0:T(8,128)(2,1)}) %all-gather.2.cloned.1.call-update) | async-done | bytes 3670032 | tf_op jit(solution)/shard_map/all_gather | solution.py:71
  406.2 4.3 %copy.19 = bf16[448,4096]{1,0:T(8,128)(2,1)} copy(bf16[448,4096]{1,0:T(8,128)(2,1)} %all-gather.2.cloned.1.call-done) | data formatting | bytes 7340032
  (13 shorter events, 0.0 us)
Async XLA Ops:
  7.2 303.3 %copy-start = (bf16[64,256]{1,0:T(8,128)(2,1)S(1)}, bf16[64,256]{1,0:T(8,128)(2,1)}, u32[]{:S(2)}) copy-start(bf16[64,256]{1,0:T(8,128)(2,1)} %param.11) | copy-start | bytes 98308
  7.2 18.6 %copy-start.1 = (s32[256]{0:T(256)S(1)}, s32[256]{0:T(256)}, u32[]{:S(2)}) copy-start(s32[256]{0:T(256)} %param.13) | copy-start | bytes 3076
  7.2 18.6 %copy-start.2 = (s32[256]{0:T(256)S(1)}, s32[256]{0:T(256)}, u32[]{:S(2)}) copy-start(s32[256]{0:T(256)} %param.12) | copy-start | bytes 3076
  7.2 18.7 %copy-start.3 = (bf16[2,256,448]{1,2,0:T(8,128)(2,1)S(1)}, bf16[2,256,448]{1,2,0:T(8,128)(2,1)}, u32[]{:S(2)}) copy-start(bf16[2,256,448]{1,2,0:T(8,128)(2,1)} %param.9) | copy-start | bytes 1376260
  9.8 71.2 %all-to-all-start = ((bf16[32,256,128]{1,2,0:T(8,128)(2,1)}), bf16[32,256,128]{1,2,0:T(8,128)(2,1)S(1)}, u32[]{:S(2)}, u32[]{:S(2)}) async-start(bf16[32,256,128]{1,2,0:T(8,128)(2,1)} %stack.2), calls=%async_computation | async-start | bytes 4194304 | tf_op jit(solution)/shard_map/all_to_all | solution.py:40
  25.7 187.7 %all-reduce.2.cloned.1.call-start = ((), (), s32[]{:S(2)}) async-start(), calls=%async_computation.3 | async-start | bytes 229376 | tf_op jit(solution)/shard_map/psum | solution.py:36
  26.9 283.5 %reduce-scatter.2.cloned.1.call-start = ((), (), s32[]{:S(2)}) async-start(), calls=%async_computation.2 | async-start | bytes 3899392 | tf_op jit(solution)/shard_map/reduce_scatter | solution.py:44
  83.9 226.5 %copy-start.4 = (s32[448,256]{1,0:T(8,128)S(1)}, s32[448,256]{1,0:T(8,128)}, u32[]{:S(2)}) copy-start(s32[448,256]{1,0:T(8,128)} %param.17) | copy-start | bytes 1376260
  83.9 226.6 %copy-start.5 = (bf16[448,256]{1,0:T(8,128)(2,1)S(1)}, bf16[448,256]{1,0:T(8,128)(2,1)}, u32[]{:S(2)}) copy-start(bf16[448,256]{1,0:T(8,128)(2,1)} %param.15) | copy-start | bytes 688132
  83.9 228.0 %copy-start.6 = (bf16[448,256]{1,0:T(8,128)(2,1)S(1)}, bf16[448,256]{1,0:T(8,128)(2,1)}, u32[]{:S(2)}) copy-start(bf16[448,256]{1,0:T(8,128)(2,1)} %param.14) | copy-start | bytes 688132
  83.9 228.0 %copy-start.7 = (bf16[448,256]{1,0:T(8,128)(2,1)S(1)}, bf16[448,256]{1,0:T(8,128)(2,1)}, u32[]{:S(2)}) copy-start(bf16[448,256]{1,0:T(8,128)(2,1)} %param.16) | copy-start | bytes 688132
  84.0 322.3 %all-gather.2.cloned.1.call-start = ((), (), s32[]{:S(2)}) async-start(), calls=%async_computation.4 | async-start | bytes 3899392 | tf_op jit(solution)/shard_map/all_gather | solution.py:71
  311.9 3.1 copy-start.8
Sparse Core Ops, SparseCore 0:
  30.0 183.3 all-reduce.1
  217.1 93.3 reduce-scatter.1
  315.1 91.0 all-gather.1
